TPU v7x, 32 devices: a whole 2x2x4 slice. The times are simulated.
32 devices in a mesh: freq: 8 (over z, y), patch: 4 (over x, core).
Axes of the slice: x: 2, y: 2, z: 4, core: 2. Of those that a mesh axis runs over, the one named last changes fastest.
Arguments:
- pressures: bfloat16 [2, 128, 131072], P(None, 'freq', 'patch'), may hold values from -6 to 6
- templates: bfloat16 [4, 128, 128], replicated, may hold values from -0.5 to 0.5
- panel_map: int32 [1024, 4], P('patch'), may hold values from 0 to 511, as said below
- blend_weights: float32 [1024, 4], P('patch'), may hold values from 0.1 to 1
- pattern_label: int32 [1024], P('patch'), may hold values from 0 to 3
- zone_ids: int32 [128, 1024], P('patch', 'freq'), may hold values from 0 to 7
- zone_gain: float32 [8], replicated, may hold values from 0.5 to 2
- stiffness: float32 [128, 1024], P('patch', 'freq'), may hold values from 0.05 to 0.5
Outputs:
- plate_stress: bfloat16 [1024, 128, 1024], P(None, 'patch', 'freq')
Inputs may be any that keep to these rules, and one draw needn't show every extreme that they name: `panel_map`: node blocks of region 0 name only values of 256 or more.
All inputs are finite; a program needn't handle non-finite values.
Results may differ from a plain program's by a relative error of at most 0.0068.
Values may be sent and summed in bfloat16 or wider, within the bound.
A program may use at most 128 MiB of HBM per device.

v0:
```python
import functools
import math

import jax
import jax.numpy as jnp
from jax import lax
from jax.experimental import pallas as pl
from jax.experimental.pallas import tpu as pltpu
from jax.sharding import PartitionSpec as P

NT = 1024
PW = 128
VMEM_LIMIT = 63 * 1024 * 1024
BF16 = jnp.bfloat16
F32 = jnp.float32


def fourier_factors(nt, fine, parts, freqs):
    def angles(clock):
        turns = clock[:, None] * freqs[None, :] % nt
        return turns.astype(F32) * (2.0 * math.pi / nt)
    coarse = angles(jnp.arange(0, nt, fine, dtype=jnp.int32))
    small = angles(jnp.arange(fine, dtype=jnp.int32))
    cosine, sine = jnp.cos(coarse), jnp.sin(coarse)
    real = parts[None, :] == 0
    return (jnp.stack([jnp.where(real, cosine, -sine), jnp.where(real, sine, cosine)]),
            jnp.stack([jnp.cos(small), jnp.sin(small)]))


def exchange_kernel(rows, groups, owners, patches, scale, map_ref, weight_ref, label_ref, gain_ref, own_ref,
                    templates_ref, zone_ref, stiff_ref, coarse_ref, fine_ref, out_ref, dft_ref,
                    blended, spectra, load, coefs, coef_ref, local_sem, press_sem, edge_sem, coef_sem, column_sem, *tables):
    pieces, cf, width = own_ref.shape
    kinds = templates_ref.shape[1] // PW
    me, patch = lax.axis_index("freq"), lax.axis_index("patch")
    has_prev, has_next = patch > 0, patch < patches - 1
    lane = lax.broadcasted_iota(jnp.int32, (groups, cf, PW), 2)
    empty = jnp.zeros((1, cf, PW), F32)

    def partner(k):
        return lax.rem(me + k, owners)

    def remote(src, dst, sems, at, **device):
        return pltpu.make_async_remote_copy(
            src_ref=src, dst_ref=dst, send_sem=sems.at[(0,) + at], recv_sem=sems.at[(1,) + at],
            device_id=device, device_id_type=pl.DeviceIdType.MESH)

    def pressure_copy(p):
        return remote(own_ref.at[p], tables[p].at[:, pl.ds(0, width)], press_sem, (p,),
                      patch=patch + 1)

    def own_copy(p):
        return pltpu.make_async_copy(
            own_ref.at[p], tables[p].at[:, pl.ds(width, width)], local_sem.at[0, p])

    def down_copy(p):
        return remote(spectra.at[p, rows], spectra.at[p, 0], edge_sem, (p, 0), patch=patch + 1)

    def up_copy(p):
        return remote(spectra.at[p, 1], spectra.at[p, rows + 1], edge_sem, (p, 1),
                      patch=patch - 1)

    def coef_copy(k, slot):
        return remote(coef_ref, coefs.at[slot], coef_sem, (k,), freq=partner(k))

    half = rows // 2
    far_first = sorted(range(1, owners), key=lambda k: -min(k, owners - k))

    def column_copy(p, h, k, slot):
        part = pl.ds(h * half, half)
        return remote(load.at[p, partner(k), part], out_ref.at[slot, p, part], column_sem,
                      (p, h, k), freq=partner(k))

    def keep_copy(p):
        return pltpu.make_async_copy(load.at[p, me], out_ref.at[me, p], local_sem.at[1, p])

    barrier = pltpu.get_barrier_semaphore()
    for k in range(1, owners):
        pl.semaphore_signal(barrier, inc=1, device_id={"freq": partner(k)},
                            device_id_type=pl.DeviceIdType.MESH)

    @pl.when(has_prev)
    def _():
        pl.semaphore_signal(barrier, inc=1, device_id={"patch": patch - 1},
                            device_id_type=pl.DeviceIdType.MESH)

    @pl.when(has_next)
    def _():
        pl.semaphore_signal(barrier, inc=1, device_id={"patch": patch + 1},
                            device_id_type=pl.DeviceIdType.MESH)

    for p in range(pieces):
        own_copy(p).start()
    gain = jnp.zeros(zone_ref.shape, F32)
    for zone in range(gain_ref.shape[0]):
        gain = jnp.where(zone_ref[...] == zone, gain_ref[zone], gain)
    gain = gain * scale
    coef_ref[0] = gain * (1.0 + 4.0 * stiff_ref[...])
    coef_ref[1] = gain * stiff_ref[...]
    pl.semaphore_wait(
        barrier, owners - 1 + has_prev.astype(jnp.int32) + has_next.astype(jnp.int32))

    @pl.when(has_next)
    def _():
        pressure_copy(0).start()

    for k in range(1, owners):
        coef_copy(k, me).start()
    coefs[me] = coef_ref[...]

    @pl.when(jnp.logical_not(has_prev))
    def _():
        for p in range(pieces):
            tables[p][:, :width] = jnp.zeros((cf, width), BF16)
            spectra[p, 0] = jnp.zeros((groups, cf, PW), BF16)

    @pl.when(jnp.logical_not(has_next))
    def _():
        for p in range(pieces):
            spectra[p, rows + 1] = jnp.zeros((groups, cf, PW), BF16)

    def table_rows(n, carry):
        values = coarse_ref[0, n][None, :] * fine_ref[0] - coarse_ref[1, n][None, :] * fine_ref[1]
        dft_ref[n] = values.astype(BF16)
        return carry

    lax.fori_loop(0, coarse_ref.shape[1], table_rows, 0)

    @pl.when(has_next)
    def _():
        for p in range(1, pieces):
            pressure_copy(p - 1).wait_send()
            pressure_copy(p).start()

    def blend_row(p, i):
        for g in range(groups):
            total = None
            for j in range(4):
                at = map_ref[j, i * groups + g] * PW
                term = tables[p][:, pl.ds(at, PW)].astype(F32) * weight_ref[j, i * groups + g]
                total = term if total is None else total + term
            blended[i, g] = total.astype(BF16)

    def map_row(p, i):
        flat = blended[i].reshape(groups * cf, PW)
        products = jnp.dot(flat, templates_ref[...], preferred_element_type=F32)
        for g in range(groups):
            label = jnp.full((1, PW), label_ref[i * groups + g], jnp.int32)
            block = products[g * cf:(g + 1) * cf]
            picked = block[:, :PW]
            for kind in range(1, kinds):
                picked = jnp.where(label == kind, block[:, kind * PW:(kind + 1) * PW], picked)
            spectra[p, i + 1, g] = picked.astype(BF16)

    def stress_row(p, i):
        here = spectra[p, i + 1].astype(F32)
        from_left = pltpu.roll(here, 1, 2)
        from_right = pltpu.roll(here, PW - 1, 2)
        left = jnp.where(lane == 0, jnp.concatenate([empty, from_left[:-1]], 0), from_left)
        right = jnp.where(
            lane == PW - 1, jnp.concatenate([from_right[1:], empty], 0), from_right)
        beside = spectra[p, i].astype(F32) + spectra[p, i + 2].astype(F32) + left + right
        centre_gain = coefs[:, 0, i][:, None, :]
        beside_gain = coefs[:, 1, i][:, None, :]
        load[p, :, i] = (centre_gain * here - beside_gain * beside).astype(BF16)

    def each(first, last, act, p, unroll):
        def body(i, carry):
            act(p, i)
            return carry
        lax.fori_loop(first, last, body, 0, unroll=unroll)

    for p in range(pieces):
        own_copy(p).wait()

        @pl.when(has_prev)
        def _():
            pressure_copy(p).wait_recv()

        for act in (blend_row, map_row):
            act(p, 0)
            act(p, rows - 1)

        @pl.when(has_prev)
        def _():
            up_copy(p).start()

        @pl.when(has_next)
        def _():
            down_copy(p).start()

        each(1, rows - 1, blend_row, p, 2)
        each(1, rows - 1, map_row, p, 3)
        if p == 0:
            for k in range(1, owners):
                coef_copy(k, lax.rem(me + owners - k, owners)).wait_recv()

        @pl.when(has_prev)
        def _():
            down_copy(p).wait_recv()

        each(0, half, stress_row, p, 2)
        for k in far_first:
            column_copy(p, 0, k, me).start()

        @pl.when(has_next)
        def _():
            up_copy(p).wait_recv()

        each(half, rows, stress_row, p, 2)
        for k in far_first:
            column_copy(p, 1, k, me).start()
        keep_copy(p).start()

    @pl.when(has_next)
    def _():
        pressure_copy(pieces - 1).wait_send()
        for p in range(pieces):
            down_copy(p).wait_send()

    @pl.when(has_prev)
    def _():
        for p in range(pieces):
            up_copy(p).wait_send()

    for k in range(1, owners):
        coef_copy(k, me).wait_send()
    for p in range(pieces):
        keep_copy(p).wait()
        for h in range(2):
            for k in range(1, owners):
                column_copy(p, h, k, me).wait_send()
                column_copy(p, h, k, lax.rem(me + owners - k, owners)).wait_recv()


def exchange(panel_map, weights, labels, zone_gain, own, templates, zone_ids, stiffness, coarse,
             fine, scale, groups, owners, patches):
    rows = zone_ids.shape[0]
    pieces, cf, width = own.shape
    smem = pl.BlockSpec(memory_space=pltpu.SMEM)
    hbm = pl.BlockSpec(memory_space=pl.ANY)
    vmem = pl.BlockSpec(memory_space=pltpu.VMEM)
    dma = pltpu.SemaphoreType.DMA
    return pl.pallas_call(
        functools.partial(exchange_kernel, rows, groups, owners, patches, scale),
        out_shape=(
            jax.ShapeDtypeStruct((owners, pieces, rows, cf, PW), BF16),
            jax.ShapeDtypeStruct((coarse.shape[1],) + fine.shape[1:], BF16),
        ),
        in_specs=[smem, smem, smem, smem, hbm, vmem, vmem, vmem, vmem, vmem],
        out_specs=(hbm, vmem),
        scratch_shapes=[
            pltpu.VMEM((rows, groups, cf, PW), BF16),
            pltpu.VMEM((pieces, rows + 2, groups, cf, PW), BF16),
            pltpu.VMEM((pieces, groups, rows, cf, PW), BF16),
            pltpu.VMEM((owners, 2, rows, PW), F32),
            pltpu.VMEM((2, rows, PW), F32),
            dma((2, pieces)),
            dma((2, pieces)),
            dma((2, pieces, 2)),
            dma((2, owners)),
            dma((2, pieces, 2, owners)),
        ] + [pltpu.VMEM((cf, 2 * width), BF16)] * pieces,
        compiler_params=pltpu.CompilerParams(
            vmem_limit_bytes=VMEM_LIMIT, collective_id=0, has_side_effects=True),
        cost_estimate=pl.CostEstimate(
            flops=2 * own.size * templates.shape[1], bytes_accessed=40 * own.size,
            transcendentals=0),
    )(panel_map, weights, labels, zone_gain, own, templates, zone_ids, stiffness, coarse, fine)


def history_kernel(rows, pieces, *refs):
    table_ref, load_ref, out_ref, wide = refs
    steps = table_ref.shape[0]
    stride = rows + 1
    for r in range(0, rows, 2):
        sides = []
        for q in (r, r + 1):
            stack = [load_ref[:, piece, q].reshape(-1, PW) for piece in range(pieces)]
            sides.append(stack[0] if pieces == 1 else jnp.concatenate(stack, 0))
        values = jnp.dot(
            table_ref[...], jnp.concatenate(sides, 1), preferred_element_type=F32)
        wide[pl.ds(r, steps, stride=stride), :] = values[:, :PW]
        wide[pl.ds(r + 1, steps, stride=stride), :] = values[:, PW:]
    for t in range(steps):
        out_ref[t] = wide[pl.ds(t * stride, rows), :].astype(BF16)


def histories(table, load):
    nt, depth = table.shape
    pieces, rows = load.shape[1:3]
    steps = 256
    whole = pl.BlockSpec(memory_space=pltpu.VMEM)
    return pl.pallas_call(
        functools.partial(history_kernel, rows, pieces),
        grid=(nt // steps,),
        out_shape=jax.ShapeDtypeStruct((nt, rows, PW), BF16),
        in_specs=[pl.BlockSpec((steps, depth), lambda t: (t, 0)), whole],
        out_specs=pl.BlockSpec((steps, rows, PW), lambda t: (t, 0, 0)),
        scratch_shapes=[pltpu.VMEM(((steps + 1) * (rows + 1), PW), F32)],
        compiler_params=pltpu.CompilerParams(vmem_limit_bytes=VMEM_LIMIT),
        cost_estimate=pl.CostEstimate(
            flops=2 * nt * depth * rows * PW, bytes_accessed=2 * nt * rows * PW,
            transcendentals=0),
    )(table, load)


def shards(
    pressures, templates, panel_map, blend_weights, pattern_label, zone_ids, zone_gain, stiffness
):
    owners = lax.axis_size("freq")
    fl = pressures.shape[1]
    nfreq = fl * owners
    rows, cols = zone_ids.shape
    groups = owners * cols // PW
    kinds = templates.shape[0]
    stacked = jnp.transpose(templates, (1, 0, 2)).reshape(PW, kinds * PW)

    pieces = 2 if fl % 16 == 0 else 1
    own = pressures.reshape(pieces, 2 * fl // pieces, pressures.shape[2])
    order = jnp.arange(2 * nfreq, dtype=jnp.int32)
    if pieces == 2:
        kind, freq = order // nfreq, order % nfreq
    else:
        kind, freq = order // fl % 2, order // (2 * fl) * fl + order % fl
    coarse, fine = fourier_factors(NT, 32, kind, freq + 1)
    load, table = exchange(
        panel_map.T, blend_weights.T, pattern_label, zone_gain, own, stacked, zone_ids, stiffness,
        coarse, fine, 1.0 / math.sqrt(nfreq), groups, owners, lax.axis_size("patch"))
    return histories(table.reshape(NT, 2 * nfreq), load)


def solution(mesh):
    placed = (
        P(None, "freq", "patch"),
        P(),
        P("patch", None),
        P("patch", None),
        P("patch"),
        P("patch", "freq"),
        P(),
        P("patch", "freq"),
    )
    return jax.shard_map(
        shards, mesh=mesh, in_specs=placed, out_specs=P(None, "patch", "freq"), check_vma=False
    )
```

profile of v0, /device:TPU:2, one launch (start us, length us, event | category | flops | bytes accessed | tf_op | source)
XLA Modules:
  0.0 76.8 jit_solution(4840325240729224099)
XLA Ops:
  0.0 0.0 copy-start
  0.0 0.3 fusion.10
  0.3 0.7 pad_maximum_fusion
  1.0 0.0 copy-done
  1.0 0.7 copy_bitcast_fusion.templates_ref
  1.6 68.0 %shard_map.82 = (bf16[8,2,32,16,128]{4,3,2,1,0:T(8,128)(2,1)}, bf16[32,32,256]{2,1,0:T(8,128)(2,1)}) custom-call(s32[4,256]{1,0:T(4,128)} %bitcast.10, f32[4,256]{1,0:T(4,128)} %bitcast.11, s32[256]{0:T(256)} %label_ref.1, f32[8]{0:T(128)} %gain_ref.1, bf16[2,16,32768]{2,1,0:T(8,128)(2,1)} %own_ref.1, bf16[128,512]{1,0:T(8,128)(2,1)} %copy_bitcast_fusion.templates_ref, ...), custom_call_target="tpu_custom_call" | custom-call | flops 1073741824 | bytes 41943040 | tf_op jit(solution)/shard_map/pallas_call | solution.py:244
  69.7 7.2 %shard_map.83 = bf16[1024,32,128]{2,1,0:T(8,128)(2,1)} custom-call(bf16[1024,256]{1,0:T(8,128)(2,1)} %bitcast.9, bf16[8,2,32,16,128]{4,3,2,1,0:T(8,128)(2,1)} %get-tuple-element.8.refs_1_), custom_call_target="tpu_custom_call" | custom-call | flops 2147483648 | bytes 8388608 | tf_op jit(solution)/shard_map/pallas_call | solution.py:294
  (3 shorter events, 0.0 us)
Async XLA Ops:
  0.0 1.0 %copy-start = (bf16[4,128,128]{2,1,0:T(8,128)(2,1)S(1)}, bf16[4,128,128]{2,1,0:T(8,128)(2,1)}, u32[]{:S(2)}) copy-start(bf16[4,128,128]{2,1,0:T(8,128)(2,1)} %param.9) | copy-start | bytes 393220
where the time goes:
time: 77 us; the launch traced here: 76.8 us
  Pallas kernels  75.2 us (98%)
  other arithmetic  0.96 us (1%)
    pallas_call x1, Pallas kernels, exchange(): pl.pallas_call(functools.partial(exchange_kernel, rows, groups, owners, p...  68 us
    pallas_call x1, Pallas kernels, histories(): pl.pallas_call(functools.partial(history_kernel, rows, pieces), grid=(nt...  7.16 us

commit v1 on v0

--- a/solution.py
+++ b/solution.py
@@ -10,35 +10,53 @@
 
 NT = 1024
 PW = 128
+GROUPS = 3
 VMEM_LIMIT = 63 * 1024 * 1024
 BF16 = jnp.bfloat16
 F32 = jnp.float32
 
 
-def fourier_factors(nt, fine, parts, freqs):
+def row_cuts(rows):
+    inner = rows - 2
+    return [1 + inner * n // GROUPS for n in range(GROUPS + 1)]
+
+
+def fourier_factors(nt, fine, nfreq, fl, whole):
+    step = lax.broadcasted_iota(jnp.int32, (fine, 2 * nfreq), 0)
+    order = lax.broadcasted_iota(jnp.int32, (fine, 2 * nfreq), 1)
+    if whole:
+        real, freq = order < nfreq, order % nfreq
+    else:
+        real, freq = order // fl % 2 == 0, order // (2 * fl) * fl + order % fl
+
     def angles(clock):
-        turns = clock[:, None] * freqs[None, :] % nt
+        turns = clock * (freq + 1) % nt
         return turns.astype(F32) * (2.0 * math.pi / nt)
-    coarse = angles(jnp.arange(0, nt, fine, dtype=jnp.int32))
-    small = angles(jnp.arange(fine, dtype=jnp.int32))
+
+    coarse, small = angles(step * fine), angles(step)
     cosine, sine = jnp.cos(coarse), jnp.sin(coarse)
-    real = parts[None, :] == 0
-    return (jnp.stack([jnp.where(real, cosine, -sine), jnp.where(real, sine, cosine)]),
-            jnp.stack([jnp.cos(small), jnp.sin(small)]))
+    return (jnp.where(real, cosine, -sine), jnp.where(real, sine, cosine),
+            jnp.cos(small), jnp.sin(small))
 
 
 def exchange_kernel(rows, groups, owners, patches, scale, map_ref, weight_ref, label_ref, gain_ref, own_ref,
-                    templates_ref, zone_ref, stiff_ref, coarse_ref, fine_ref, out_ref, dft_ref,
-                    blended, spectra, load, coefs, coef_ref, local_sem, press_sem, edge_sem, coef_sem, column_sem, *tables):
+                    templates_ref, zone_ref, stiff_ref, out_ref, dft_ref,
+                    blended, spectra, load, coefs, coef_ref, stacked, factors, local_sem, press_sem, edge_sem,
+                    coef_sem, column_sem, *tables):
     pieces, cf, width = own_ref.shape
-    kinds = templates_ref.shape[1] // PW
+    kinds = templates_ref.shape[0]
     me, patch = lax.axis_index("freq"), lax.axis_index("patch")
     has_prev, has_next = patch > 0, patch < patches - 1
     lane = lax.broadcasted_iota(jnp.int32, (groups, cf, PW), 2)
     empty = jnp.zeros((1, cf, PW), F32)
+    cuts = row_cuts(rows)
+    far_first = sorted(range(1, owners), key=lambda k: -min(k, owners - k))
 
     def partner(k):
         return lax.rem(me + k, owners)
+
+    def source(k):
+        return lax.rem(me + owners - k, owners)
 
     def remote(src, dst, sems, at, **device):
         return pltpu.make_async_remote_copy(
@@ -51,7 +69,7 @@
 
     def own_copy(p):
         return pltpu.make_async_copy(
-            own_ref.at[p], tables[p].at[:, pl.ds(width, width)], local_sem.at[0, p])
+            own_ref.at[p], tables[p].at[:, pl.ds(width, width)], local_sem.at[p])
 
     def down_copy(p):
         return remote(spectra.at[p, rows], spectra.at[p, 0], edge_sem, (p, 0), patch=patch + 1)
@@ -63,16 +81,18 @@
     def coef_copy(k, slot):
         return remote(coef_ref, coefs.at[slot], coef_sem, (k,), freq=partner(k))
 
-    half = rows // 2
-    far_first = sorted(range(1, owners), key=lambda k: -min(k, owners - k))
-
-    def column_copy(p, h, k, slot):
-        part = pl.ds(h * half, half)
-        return remote(load.at[p, partner(k), part], out_ref.at[slot, p, part], column_sem,
-                      (p, h, k), freq=partner(k))
-
-    def keep_copy(p):
-        return pltpu.make_async_copy(load.at[p, me], out_ref.at[me, p], local_sem.at[1, p])
+    def inner_copy(p, n, k, slot):
+        part = pl.ds(cuts[n] - 1, cuts[n + 1] - cuts[n])
+        return remote(load.at[partner(k), p, part], out_ref.at[slot, p, part], column_sem,
+                      (p * GROUPS + n, k), freq=partner(k))
+
+    def outer_copy(k, slot):
+        part = pl.ds(rows - 2, 2)
+        return remote(load.at[partner(k), :, part], out_ref.at[slot, :, part], column_sem,
+                      (pieces * GROUPS, k), freq=partner(k))
+
+    def keep_copy():
+        return pltpu.make_async_copy(load.at[me], out_ref.at[me], local_sem.at[pieces])
 
     barrier = pltpu.get_barrier_semaphore()
     for k in range(1, owners):
@@ -107,6 +127,8 @@
     for k in range(1, owners):
         coef_copy(k, me).start()
     coefs[me] = coef_ref[...]
+    for kind in range(kinds):
+        stacked[:, kind * PW:(kind + 1) * PW] = templates_ref[kind]
 
     @pl.when(jnp.logical_not(has_prev))
     def _():
@@ -118,19 +140,6 @@
     def _():
         for p in range(pieces):
             spectra[p, rows + 1] = jnp.zeros((groups, cf, PW), BF16)
-
-    def table_rows(n, carry):
-        values = coarse_ref[0, n][None, :] * fine_ref[0] - coarse_ref[1, n][None, :] * fine_ref[1]
-        dft_ref[n] = values.astype(BF16)
-        return carry
-
-    lax.fori_loop(0, coarse_ref.shape[1], table_rows, 0)
-
-    @pl.when(has_next)
-    def _():
-        for p in range(1, pieces):
-            pressure_copy(p - 1).wait_send()
-            pressure_copy(p).start()
 
     def blend_row(p, i):
         for g in range(groups):
@@ -143,7 +152,7 @@
 
     def map_row(p, i):
         flat = blended[i].reshape(groups * cf, PW)
-        products = jnp.dot(flat, templates_ref[...], preferred_element_type=F32)
+        products = jnp.dot(flat, stacked[...], preferred_element_type=F32)
         for g in range(groups):
             label = jnp.full((1, PW), label_ref[i * groups + g], jnp.int32)
             block = products[g * cf:(g + 1) * cf]
@@ -152,7 +161,7 @@
                 picked = jnp.where(label == kind, block[:, kind * PW:(kind + 1) * PW], picked)
             spectra[p, i + 1, g] = picked.astype(BF16)
 
-    def stress_row(p, i):
+    def stress_row(p, i, at):
         here = spectra[p, i + 1].astype(F32)
         from_left = pltpu.roll(here, 1, 2)
         from_right = pltpu.roll(here, PW - 1, 2)
@@ -162,7 +171,10 @@
         beside = spectra[p, i].astype(F32) + spectra[p, i + 2].astype(F32) + left + right
         centre_gain = coefs[:, 0, i][:, None, :]
         beside_gain = coefs[:, 1, i][:, None, :]
-        load[p, :, i] = (centre_gain * here - beside_gain * beside).astype(BF16)
+        load[:, p, at] = (centre_gain * here - beside_gain * beside).astype(BF16)
+
+    def inner_stress(p, i):
+        stress_row(p, i, i - 1)
 
     def each(first, last, act, p, unroll):
         def body(i, carry):
@@ -189,32 +201,52 @@
         def _():
             down_copy(p).start()
 
-        each(1, rows - 1, blend_row, p, 2)
-        each(1, rows - 1, map_row, p, 3)
-        if p == 0:
-            for k in range(1, owners):
-                coef_copy(k, lax.rem(me + owners - k, owners)).wait_recv()
-
+        for n in range(GROUPS):
+            first = cuts[n] + (n > 0)
+            last = min(cuts[n + 1] + 1, rows - 1)
+            each(first, last, blend_row, p, 2)
+            each(first, last, map_row, p, 3)
+            if p == 0 and n == 0:
+                for k in range(1, owners):
+                    coef_copy(k, source(k)).wait_recv()
+            each(cuts[n], cuts[n + 1], inner_stress, p, 2)
+            for k in far_first:
+                inner_copy(p, n, k, me).start()
+
+        @pl.when(has_next)
+        def _():
+            pressure_copy(p).wait_send()
+            if p + 1 < pieces:
+                pressure_copy(p + 1).start()
+
+    for p in range(pieces):
         @pl.when(has_prev)
         def _():
             down_copy(p).wait_recv()
 
-        each(0, half, stress_row, p, 2)
-        for k in far_first:
-            column_copy(p, 0, k, me).start()
-
         @pl.when(has_next)
         def _():
             up_copy(p).wait_recv()
 
-        each(half, rows, stress_row, p, 2)
-        for k in far_first:
-            column_copy(p, 1, k, me).start()
-        keep_copy(p).start()
+        stress_row(p, 0, rows - 2)
+        stress_row(p, rows - 1, rows - 1)
+    for k in far_first:
+        outer_copy(k, me).start()
+    keep_copy().start()
+
+    for n, values in enumerate(
+            fourier_factors(NT, factors.shape[1], factors.shape[2] // 2, cf * pieces // 2, pieces == 2)):
+        factors[n] = values
+
+    def table_rows(n, carry):
+        values = (factors[0, pl.ds(n, 1)] * factors[2] - factors[1, pl.ds(n, 1)] * factors[3])
+        dft_ref[n] = values.astype(BF16)
+        return carry
+
+    lax.fori_loop(0, factors.shape[1], table_rows, 0)
 
     @pl.when(has_next)
     def _():
-        pressure_copy(pieces - 1).wait_send()
         for p in range(pieces):
             down_copy(p).wait_send()
 
@@ -225,18 +257,23 @@
 
     for k in range(1, owners):
         coef_copy(k, me).wait_send()
-    for p in range(pieces):
-        keep_copy(p).wait()
-        for h in range(2):
-            for k in range(1, owners):
-                column_copy(p, h, k, me).wait_send()
-                column_copy(p, h, k, lax.rem(me + owners - k, owners)).wait_recv()
-
-
-def exchange(panel_map, weights, labels, zone_gain, own, templates, zone_ids, stiffness, coarse,
-             fine, scale, groups, owners, patches):
+    keep_copy().wait()
+    for k in range(1, owners):
+        for p in range(pieces):
+            for n in range(GROUPS):
+                inner_copy(p, n, k, me).wait_send()
+                inner_copy(p, n, k, source(k)).wait_recv()
+        outer_copy(k, me).wait_send()
+        outer_copy(k, source(k)).wait_recv()
+
+
+def exchange(panel_map, weights, labels, zone_gain, own, templates, zone_ids, stiffness, scale,
+             groups, owners, patches):
     rows = zone_ids.shape[0]
     pieces, cf, width = own.shape
+    kinds = templates.shape[0]
+    depth = owners * pieces * cf
+    fine = math.isqrt(NT)
     smem = pl.BlockSpec(memory_space=pltpu.SMEM)
     hbm = pl.BlockSpec(memory_space=pl.ANY)
     vmem = pl.BlockSpec(memory_space=pltpu.VMEM)
@@ -245,28 +282,30 @@
         functools.partial(exchange_kernel, rows, groups, owners, patches, scale),
         out_shape=(
             jax.ShapeDtypeStruct((owners, pieces, rows, cf, PW), BF16),
-            jax.ShapeDtypeStruct((coarse.shape[1],) + fine.shape[1:], BF16),
+            jax.ShapeDtypeStruct((fine, fine, depth), BF16),
         ),
-        in_specs=[smem, smem, smem, smem, hbm, vmem, vmem, vmem, vmem, vmem],
+        in_specs=[smem, smem, smem, smem, hbm, vmem, vmem, vmem],
         out_specs=(hbm, vmem),
         scratch_shapes=[
             pltpu.VMEM((rows, groups, cf, PW), BF16),
             pltpu.VMEM((pieces, rows + 2, groups, cf, PW), BF16),
-            pltpu.VMEM((pieces, groups, rows, cf, PW), BF16),
+            pltpu.VMEM((groups, pieces, rows, cf, PW), BF16),
             pltpu.VMEM((owners, 2, rows, PW), F32),
             pltpu.VMEM((2, rows, PW), F32),
-            dma((2, pieces)),
+            pltpu.VMEM((PW, kinds * PW), BF16),
+            pltpu.VMEM((4, fine, depth), F32),
+            dma((pieces + 1,)),
             dma((2, pieces)),
             dma((2, pieces, 2)),
             dma((2, owners)),
-            dma((2, pieces, 2, owners)),
+            dma((2, pieces * GROUPS + 1, owners)),
         ] + [pltpu.VMEM((cf, 2 * width), BF16)] * pieces,
         compiler_params=pltpu.CompilerParams(
             vmem_limit_bytes=VMEM_LIMIT, collective_id=0, has_side_effects=True),
         cost_estimate=pl.CostEstimate(
-            flops=2 * own.size * templates.shape[1], bytes_accessed=40 * own.size,
+            flops=2 * own.size * kinds * PW, bytes_accessed=40 * own.size,
             transcendentals=0),
-    )(panel_map, weights, labels, zone_gain, own, templates, zone_ids, stiffness, coarse, fine)
+    )(panel_map, weights, labels, zone_gain, own, templates, zone_ids, stiffness)
 
 
 def history_kernel(rows, pieces, *refs):
@@ -276,7 +315,8 @@
     for r in range(0, rows, 2):
         sides = []
         for q in (r, r + 1):
-            stack = [load_ref[:, piece, q].reshape(-1, PW) for piece in range(pieces)]
+            at = q - 1 if 0 < q < rows - 1 else rows - 2 + (q > 0)
+            stack = [load_ref[:, piece, at].reshape(-1, PW) for piece in range(pieces)]
             sides.append(stack[0] if pieces == 1 else jnp.concatenate(stack, 0))
         values = jnp.dot(
             table_ref[...], jnp.concatenate(sides, 1), preferred_element_type=F32)
@@ -313,20 +353,12 @@
     nfreq = fl * owners
     rows, cols = zone_ids.shape
     groups = owners * cols // PW
-    kinds = templates.shape[0]
-    stacked = jnp.transpose(templates, (1, 0, 2)).reshape(PW, kinds * PW)
 
     pieces = 2 if fl % 16 == 0 else 1
     own = pressures.reshape(pieces, 2 * fl // pieces, pressures.shape[2])
-    order = jnp.arange(2 * nfreq, dtype=jnp.int32)
-    if pieces == 2:
-        kind, freq = order // nfreq, order % nfreq
-    else:
-        kind, freq = order // fl % 2, order // (2 * fl) * fl + order % fl
-    coarse, fine = fourier_factors(NT, 32, kind, freq + 1)
     load, table = exchange(
-        panel_map.T, blend_weights.T, pattern_label, zone_gain, own, stacked, zone_ids, stiffness,
-        coarse, fine, 1.0 / math.sqrt(nfreq), groups, owners, lax.axis_size("patch"))
+        panel_map.T, blend_weights.T, pattern_label, zone_gain, own, templates, zone_ids, stiffness,
+        1.0 / math.sqrt(nfreq), groups, owners, lax.axis_size("patch"))
     return histories(table.reshape(NT, 2 * nfreq), load)
 
 

time: 77 us -> 69.7 us (0.905)
  the two profiles are of different devices: /device:TPU:2 before, /device:TPU:0 now
where the time goes in v1:
time: 69.7 us; the launch traced here: 69.5 us
  Pallas kernels  69.5 us (100%)
    pallas_call x1, Pallas kernels, exchange(): pl.pallas_call(functools.partial(exchange_kernel, rows, groups, owners, p...  62.4 us
    pallas_call x1, Pallas kernels, histories(): pl.pallas_call(functools.partial(history_kernel, rows, pieces), grid=(nt...  7.16 us

profile of v1, /device:TPU:0, one launch (start us, length us, event | category | flops | bytes accessed | tf_op | source)
XLA Modules:
  0.0 69.5 jit_solution(8909635491999265984)
XLA Ops:
  0.0 62.4 %shard_map.82 = (bf16[8,2,32,16,128]{4,3,2,1,0:T(8,128)(2,1)}, bf16[32,32,256]{2,1,0:T(8,128)(2,1)}) custom-call(s32[4,256]{1,0:T(4,128)} %bitcast.4, f32[4,256]{1,0:T(4,128)} %bitcast.5, s32[256]{0:T(256)} %label_ref.1, f32[8]{0:T(128)} %gain_ref.1, bf16[2,16,32768]{2,1,0:T(8,128)(2,1)} %own_ref.1, bf16[4,128,128]{2,1,0:T(8,128)(2,1)} %templates_ref.1, ...), custom_call_target="tpu_custom_call" | custom-call | flops 1073741824 | bytes 41943040 | tf_op jit(solution)/shard_map/pallas_call | solution.py:281
  62.4 7.2 %shard_map.83 = bf16[1024,32,128]{2,1,0:T(8,128)(2,1)} custom-call(bf16[1024,256]{1,0:T(8,128)(2,1)} %bitcast.3, bf16[8,2,32,16,128]{4,3,2,1,0:T(8,128)(2,1)} %get-tuple-element.8.refs_1_), custom_call_target="tpu_custom_call" | custom-call | flops 2147483648 | bytes 8388608 | tf_op jit(solution)/shard_map/pallas_call | solution.py:334

commit v2 on v1

--- a/solution.py
+++ b/solution.py
@@ -10,15 +10,18 @@
 
 NT = 1024
 PW = 128
-GROUPS = 3
-VMEM_LIMIT = 63 * 1024 * 1024
+BLOCK = 128
+SHARES = (0, 2, 6, 10, 14)
+GROUPS = len(SHARES) - 1
+VMEM_LIMIT = 40 * 1024 * 1024
+FINISH_LIMIT = 16 * 1024 * 1024
 BF16 = jnp.bfloat16
 F32 = jnp.float32
 
 
 def row_cuts(rows):
-    inner = rows - 2
-    return [1 + inner * n // GROUPS for n in range(GROUPS + 1)]
+    pairs = (rows - 2) // 2
+    return [1 + 2 * (pairs * share // SHARES[-1]) for share in SHARES]
 
 
 def fourier_factors(nt, fine, nfreq, fl, whole):
@@ -39,10 +42,10 @@
             jnp.cos(small), jnp.sin(small))
 
 
-def exchange_kernel(rows, groups, owners, patches, scale, map_ref, weight_ref, label_ref, gain_ref, own_ref,
-                    templates_ref, zone_ref, stiff_ref, out_ref, dft_ref,
-                    blended, spectra, load, coefs, coef_ref, stacked, factors, local_sem, press_sem, edge_sem,
-                    coef_sem, column_sem, *tables):
+def exchange_kernel(rows, groups, owners, patches, map_ref, weight_ref, label_ref, own_ref,
+                    templates_ref, stiff_ref, wide_ref,
+                    blended, spectra, load, arrived, own_stiff, stiffs, bending, stacked, factors, table,
+                    local_sem, press_sem, edge_sem, stiff_sem, column_sem, *tables):
     pieces, cf, width = own_ref.shape
     kinds = templates_ref.shape[0]
     me, patch = lax.axis_index("freq"), lax.axis_index("patch")
@@ -78,21 +81,21 @@
         return remote(spectra.at[p, 1], spectra.at[p, rows + 1], edge_sem, (p, 1),
                       patch=patch - 1)
 
-    def coef_copy(k, slot):
-        return remote(coef_ref, coefs.at[slot], coef_sem, (k,), freq=partner(k))
+    def stiff_copy(k, slot):
+        return remote(own_stiff, stiffs.at[slot], stiff_sem, (k,), freq=partner(k))
 
     def inner_copy(p, n, k, slot):
         part = pl.ds(cuts[n] - 1, cuts[n + 1] - cuts[n])
-        return remote(load.at[partner(k), p, part], out_ref.at[slot, p, part], column_sem,
+        return remote(load.at[partner(k), p, part], arrived.at[slot, p, part], column_sem,
                       (p * GROUPS + n, k), freq=partner(k))
 
     def outer_copy(k, slot):
         part = pl.ds(rows - 2, 2)
-        return remote(load.at[partner(k), :, part], out_ref.at[slot, :, part], column_sem,
+        return remote(load.at[partner(k), :, part], arrived.at[slot, :, part], column_sem,
                       (pieces * GROUPS, k), freq=partner(k))
 
     def keep_copy():
-        return pltpu.make_async_copy(load.at[me], out_ref.at[me], local_sem.at[pieces])
+        return pltpu.make_async_copy(load.at[me], arrived.at[me], local_sem.at[pieces])
 
     barrier = pltpu.get_barrier_semaphore()
     for k in range(1, owners):
@@ -111,12 +114,7 @@
 
     for p in range(pieces):
         own_copy(p).start()
-    gain = jnp.zeros(zone_ref.shape, F32)
-    for zone in range(gain_ref.shape[0]):
-        gain = jnp.where(zone_ref[...] == zone, gain_ref[zone], gain)
-    gain = gain * scale
-    coef_ref[0] = gain * (1.0 + 4.0 * stiff_ref[...])
-    coef_ref[1] = gain * stiff_ref[...]
+    own_stiff[...] = stiff_ref[...].astype(BF16)
     pl.semaphore_wait(
         barrier, owners - 1 + has_prev.astype(jnp.int32) + has_next.astype(jnp.int32))
 
@@ -125,8 +123,8 @@
         pressure_copy(0).start()
 
     for k in range(1, owners):
-        coef_copy(k, me).start()
-    coefs[me] = coef_ref[...]
+        stiff_copy(k, me).start()
+    stiffs[me] = own_stiff[...]
     for kind in range(kinds):
         stacked[:, kind * PW:(kind + 1) * PW] = templates_ref[kind]
 
@@ -169,9 +167,7 @@
         right = jnp.where(
             lane == PW - 1, jnp.concatenate([from_right[1:], empty], 0), from_right)
         beside = spectra[p, i].astype(F32) + spectra[p, i + 2].astype(F32) + left + right
-        centre_gain = coefs[:, 0, i][:, None, :]
-        beside_gain = coefs[:, 1, i][:, None, :]
-        load[:, p, at] = (centre_gain * here - beside_gain * beside).astype(BF16)
+        load[:, p, at] = (here + bending[:, i][:, None, :] * (4.0 * here - beside)).astype(BF16)
 
     def inner_stress(p, i):
         stress_row(p, i, i - 1)
@@ -208,7 +204,8 @@
             each(first, last, map_row, p, 3)
             if p == 0 and n == 0:
                 for k in range(1, owners):
-                    coef_copy(k, source(k)).wait_recv()
+                    stiff_copy(k, source(k)).wait_recv()
+                bending[...] = stiffs[...].astype(F32)
             each(cuts[n], cuts[n + 1], inner_stress, p, 2)
             for k in far_first:
                 inner_copy(p, n, k, me).start()
@@ -218,6 +215,17 @@
             pressure_copy(p).wait_send()
             if p + 1 < pieces:
                 pressure_copy(p + 1).start()
+
+    for n, values in enumerate(
+            fourier_factors(NT, factors.shape[1], factors.shape[2] // 2, cf * pieces // 2, pieces == 2)):
+        factors[n] = values
+
+    def table_rows(n, carry):
+        values = (factors[0, pl.ds(n, 1)] * factors[2] - factors[1, pl.ds(n, 1)] * factors[3])
+        table[n] = values.astype(BF16)
+        return carry
+
+    lax.fori_loop(0, factors.shape[1], table_rows, 0)
 
     for p in range(pieces):
         @pl.when(has_prev)
@@ -234,16 +242,38 @@
         outer_copy(k, me).start()
     keep_copy().start()
 
-    for n, values in enumerate(
-            fourier_factors(NT, factors.shape[1], factors.shape[2] // 2, cf * pieces // 2, pieces == 2)):
-        factors[n] = values
-
-    def table_rows(n, carry):
-        values = (factors[0, pl.ds(n, 1)] * factors[2] - factors[1, pl.ds(n, 1)] * factors[3])
-        dft_ref[n] = values.astype(BF16)
-        return carry
-
-    lax.fori_loop(0, factors.shape[1], table_rows, 0)
+    def history_pair(q, row, step):
+        sides = []
+        for at in (q, q + 1):
+            stack = [arrived[:, p, at].reshape(-1, PW) for p in range(pieces)]
+            sides.append(stack[0] if pieces == 1 else jnp.concatenate(stack, 0))
+        sides = jnp.concatenate(sides, 1)
+        depth = sides.shape[0]
+        per = 2 * BLOCK // table.shape[1]
+        for n in range(NT // (2 * BLOCK)):
+            part = table[n * per:(n + 1) * per].reshape(2 * BLOCK, depth)
+            values = jnp.dot(part, sides, preferred_element_type=F32)
+            for h in range(2):
+                for side in range(2):
+                    wide_ref[2 * n + h, pl.ds(row + side * step, BLOCK, stride=rows + 1), :] = (
+                        values[h * BLOCK:(h + 1) * BLOCK, side * PW:(side + 1) * PW])
+
+    keep_copy().wait()
+    for n in range(GROUPS):
+        for k in range(1, owners):
+            for p in range(pieces):
+                inner_copy(p, n, k, source(k)).wait_recv()
+
+        def inner_pair(m, carry):
+            q = cuts[n] - 1 + 2 * m
+            history_pair(q, q + 1, 1)
+            return carry
+
+        lax.fori_loop(0, (cuts[n + 1] - cuts[n]) // 2, inner_pair, 0)
+
+    for k in range(1, owners):
+        outer_copy(k, source(k)).wait_recv()
+    history_pair(rows - 2, 0, rows - 1)
 
     @pl.when(has_next)
     def _():
@@ -256,20 +286,15 @@
             up_copy(p).wait_send()
 
     for k in range(1, owners):
-        coef_copy(k, me).wait_send()
-    keep_copy().wait()
-    for k in range(1, owners):
+        stiff_copy(k, me).wait_send()
         for p in range(pieces):
             for n in range(GROUPS):
                 inner_copy(p, n, k, me).wait_send()
-                inner_copy(p, n, k, source(k)).wait_recv()
         outer_copy(k, me).wait_send()
-        outer_copy(k, source(k)).wait_recv()
-
-
-def exchange(panel_map, weights, labels, zone_gain, own, templates, zone_ids, stiffness, scale,
-             groups, owners, patches):
-    rows = zone_ids.shape[0]
+
+
+def exchange(panel_map, weights, labels, own, templates, stiffness, groups, owners, patches):
+    rows = stiffness.shape[0]
     pieces, cf, width = own.shape
     kinds = templates.shape[0]
     depth = owners * pieces * cf
@@ -279,21 +304,21 @@
     vmem = pl.BlockSpec(memory_space=pltpu.VMEM)
     dma = pltpu.SemaphoreType.DMA
     return pl.pallas_call(
-        functools.partial(exchange_kernel, rows, groups, owners, patches, scale),
-        out_shape=(
-            jax.ShapeDtypeStruct((owners, pieces, rows, cf, PW), BF16),
-            jax.ShapeDtypeStruct((fine, fine, depth), BF16),
-        ),
-        in_specs=[smem, smem, smem, smem, hbm, vmem, vmem, vmem],
-        out_specs=(hbm, vmem),
+        functools.partial(exchange_kernel, rows, groups, owners, patches),
+        out_shape=pltpu.VMEM((NT // BLOCK, BLOCK * (rows + 1), PW), F32),
+        in_specs=[smem, smem, smem, hbm, vmem, vmem],
+        out_specs=vmem,
         scratch_shapes=[
             pltpu.VMEM((rows, groups, cf, PW), BF16),
             pltpu.VMEM((pieces, rows + 2, groups, cf, PW), BF16),
             pltpu.VMEM((groups, pieces, rows, cf, PW), BF16),
-            pltpu.VMEM((owners, 2, rows, PW), F32),
-            pltpu.VMEM((2, rows, PW), F32),
+            pltpu.VMEM((owners, pieces, rows, cf, PW), BF16),
+            pltpu.VMEM((rows, PW), BF16),
+            pltpu.VMEM((owners, rows, PW), BF16),
+            pltpu.VMEM((owners, rows, PW), F32),
             pltpu.VMEM((PW, kinds * PW), BF16),
             pltpu.VMEM((4, fine, depth), F32),
+            pltpu.VMEM((fine, fine, depth), BF16),
             dma((pieces + 1,)),
             dma((2, pieces)),
             dma((2, pieces, 2)),
@@ -303,46 +328,36 @@
         compiler_params=pltpu.CompilerParams(
             vmem_limit_bytes=VMEM_LIMIT, collective_id=0, has_side_effects=True),
         cost_estimate=pl.CostEstimate(
-            flops=2 * own.size * kinds * PW, bytes_accessed=40 * own.size,
-            transcendentals=0),
-    )(panel_map, weights, labels, zone_gain, own, templates, zone_ids, stiffness)
-
-
-def history_kernel(rows, pieces, *refs):
-    table_ref, load_ref, out_ref, wide = refs
-    steps = table_ref.shape[0]
-    stride = rows + 1
-    for r in range(0, rows, 2):
-        sides = []
-        for q in (r, r + 1):
-            at = q - 1 if 0 < q < rows - 1 else rows - 2 + (q > 0)
-            stack = [load_ref[:, piece, at].reshape(-1, PW) for piece in range(pieces)]
-            sides.append(stack[0] if pieces == 1 else jnp.concatenate(stack, 0))
-        values = jnp.dot(
-            table_ref[...], jnp.concatenate(sides, 1), preferred_element_type=F32)
-        wide[pl.ds(r, steps, stride=stride), :] = values[:, :PW]
-        wide[pl.ds(r + 1, steps, stride=stride), :] = values[:, PW:]
-    for t in range(steps):
-        out_ref[t] = wide[pl.ds(t * stride, rows), :].astype(BF16)
-
-
-def histories(table, load):
-    nt, depth = table.shape
-    pieces, rows = load.shape[1:3]
-    steps = 256
-    whole = pl.BlockSpec(memory_space=pltpu.VMEM)
+            flops=2 * own.size * kinds * PW + 2 * NT * depth * rows * PW,
+            bytes_accessed=40 * own.size, transcendentals=0),
+    )(panel_map, weights, labels, own, templates, stiffness)
+
+
+def finish_kernel(scale, gain_ref, zone_ref, wide_ref, out_ref):
+    rows = zone_ref.shape[0]
+    gain = jnp.zeros(zone_ref.shape, F32)
+    for zone in range(gain_ref.shape[0]):
+        gain = jnp.where(zone_ref[...] == zone, gain_ref[zone], gain)
+    gain = gain * scale
+    block = pl.program_id(0)
+    for t in range(BLOCK):
+        values = wide_ref[block, pl.ds(t * (rows + 1), rows), :]
+        out_ref[t] = (values * gain).astype(BF16)
+
+
+def finish(wide, zone_gain, zone_ids, scale):
+    rows = zone_ids.shape[0]
     return pl.pallas_call(
-        functools.partial(history_kernel, rows, pieces),
-        grid=(nt // steps,),
-        out_shape=jax.ShapeDtypeStruct((nt, rows, PW), BF16),
-        in_specs=[pl.BlockSpec((steps, depth), lambda t: (t, 0)), whole],
-        out_specs=pl.BlockSpec((steps, rows, PW), lambda t: (t, 0, 0)),
-        scratch_shapes=[pltpu.VMEM(((steps + 1) * (rows + 1), PW), F32)],
-        compiler_params=pltpu.CompilerParams(vmem_limit_bytes=VMEM_LIMIT),
+        functools.partial(finish_kernel, scale),
+        grid=(NT // BLOCK,),
+        out_shape=jax.ShapeDtypeStruct((NT, rows, PW), BF16),
+        in_specs=[pl.BlockSpec(memory_space=pltpu.SMEM), pl.BlockSpec(memory_space=pltpu.VMEM),
+                  pl.BlockSpec(memory_space=pltpu.VMEM)],
+        out_specs=pl.BlockSpec((BLOCK, rows, PW), lambda t: (t, 0, 0)),
+        compiler_params=pltpu.CompilerParams(vmem_limit_bytes=FINISH_LIMIT),
         cost_estimate=pl.CostEstimate(
-            flops=2 * nt * depth * rows * PW, bytes_accessed=2 * nt * rows * PW,
-            transcendentals=0),
-    )(table, load)
+            flops=NT * rows * PW, bytes_accessed=2 * NT * rows * PW, transcendentals=0),
+    )(zone_gain, zone_ids, pltpu.with_memory_space_constraint(wide, pltpu.VMEM))
 
 
 def shards(
@@ -356,10 +371,10 @@
 
     pieces = 2 if fl % 16 == 0 else 1
     own = pressures.reshape(pieces, 2 * fl // pieces, pressures.shape[2])
-    load, table = exchange(
-        panel_map.T, blend_weights.T, pattern_label, zone_gain, own, templates, zone_ids, stiffness,
-        1.0 / math.sqrt(nfreq), groups, owners, lax.axis_size("patch"))
-    return histories(table.reshape(NT, 2 * nfreq), load)
+    wide = exchange(
+        panel_map.T, blend_weights.T, pattern_label, own, templates, stiffness, groups, owners,
+        lax.axis_size("patch"))
+    return finish(wide, zone_gain, zone_ids, 1.0 / math.sqrt(nfreq))
 
 
 def solution(mesh):

time: 69.7 us -> 65.3 us (0.937)
  the two profiles are of different devices: /device:TPU:0 before, /device:TPU:2 now
where the time goes in v2:
time: 65.3 us; the launch traced here: 64.1 us
  Pallas kernels  64 us (98%)
    pallas_call x1, Pallas kernels, exchange(): pl.pallas_call(functools.partial(exchange_kernel, rows, groups, owners, p...  58.7 us
    pallas_call x1, Pallas kernels, finish(): pl.pallas_call(functools.partial(finish_kernel, scale), grid=(NT // BLOCK...  5.29 us

profile of v2, /device:TPU:2, one launch (start us, length us, event | category | flops | bytes accessed | tf_op | source)
XLA Modules:
  0.0 64.1 jit_solution(7459084311793090130)
XLA Ops:
  0.0 0.0 copy-start
  0.0 0.0 copy-start.1
  0.0 58.7 %shard_map.82.wide_ref = f32[8,4224,128]{2,1,0:T(8,128)S(1)} custom-call(s32[4,256]{1,0:T(4,128)} %bitcast.2, f32[4,256]{1,0:T(4,128)} %bitcast.3, s32[256]{0:T(256)} %label_ref.1, bf16[2,16,32768]{2,1,0:T(8,128)(2,1)} %own_ref.1, bf16[4,128,128]{2,1,0:T(8,128)(2,1)} %templates_ref.1, f32[32,128]{1,0:T(8,128)} %stiff_ref.1), custom_call_target="tpu_custom_call" | custom-call | flops 3221225472 | bytes 41943040 | tf_op jit(solution)/shard_map/pallas_call | solution.py:306
  58.7 0.0 copy-done
  58.8 0.0 copy-done.1
  58.8 5.3 %shard_map.83 = bf16[1024,32,128]{2,1,0:T(8,128)(2,1)} custom-call(f32[8]{0:T(128)S(1)} %copy-done.1, s32[32,128]{1,0:T(8,128)S(1)} %copy-done, f32[8,4224,128]{2,1,0:T(8,128)S(1)} %shard_map.82.wide_ref), custom_call_target="tpu_custom_call" | custom-call | flops 4194304 | bytes 8388608 | tf_op jit(solution)/shard_map/pallas_call | solution.py:350
Async XLA Ops:
  0.0 58.7 %copy-start = (s32[32,128]{1,0:T(8,128)S(1)}, s32[32,128]{1,0:T(8,128)}, u32[]{:S(2)}) copy-start(s32[32,128]{1,0:T(8,128)} %zone_ref.1) | copy-start | bytes 49156
  0.0 58.8 %copy-start.1 = (f32[8]{0:T(128)S(1)}, f32[8]{0:T(128)}, u32[]{:S(2)}) copy-start(f32[8]{0:T(128)} %gain_ref.1) | copy-start | bytes 100

commit v3 on v2

--- a/solution.py
+++ b/solution.py
@@ -11,17 +11,18 @@
 NT = 1024
 PW = 128
 BLOCK = 128
-SHARES = (0, 2, 6, 10, 14)
-GROUPS = len(SHARES) - 1
+DEEP = 8
+FIRST_SHARES = (0, 2, 7, 15)
+LAST_SHARES = (0, 7, 15)
 VMEM_LIMIT = 40 * 1024 * 1024
 FINISH_LIMIT = 16 * 1024 * 1024
 BF16 = jnp.bfloat16
 F32 = jnp.float32
 
 
-def row_cuts(rows):
+def row_cuts(rows, shares):
     pairs = (rows - 2) // 2
-    return [1 + 2 * (pairs * share // SHARES[-1]) for share in SHARES]
+    return [1 + 2 * (pairs * share // shares[-1]) for share in shares]
 
 
 def fourier_factors(nt, fine, nfreq, fl, whole):
@@ -52,7 +53,8 @@
     has_prev, has_next = patch > 0, patch < patches - 1
     lane = lax.broadcasted_iota(jnp.int32, (groups, cf, PW), 2)
     empty = jnp.zeros((1, cf, PW), F32)
-    cuts = row_cuts(rows)
+    cuts = [row_cuts(rows, LAST_SHARES if p == pieces - 1 else FIRST_SHARES) for p in range(pieces)]
+    offsets = [sum(len(c) - 1 for c in cuts[:p]) for p in range(pieces + 1)]
     far_first = sorted(range(1, owners), key=lambda k: -min(k, owners - k))
 
     def partner(k):
@@ -84,15 +86,17 @@
     def stiff_copy(k, slot):
         return remote(own_stiff, stiffs.at[slot], stiff_sem, (k,), freq=partner(k))
 
-    def inner_copy(p, n, k, slot):
-        part = pl.ds(cuts[n] - 1, cuts[n + 1] - cuts[n])
+    def column_copy(p, n, k, slot):
+        part = pl.ds(cuts[p][n] - 1, cuts[p][n + 1] - cuts[p][n])
         return remote(load.at[partner(k), p, part], arrived.at[slot, p, part], column_sem,
-                      (p * GROUPS + n, k), freq=partner(k))
-
-    def outer_copy(k, slot):
+                      (offsets[p] + n, k), freq=partner(k))
+
+    def edge_copy(k, slot):
         part = pl.ds(rows - 2, 2)
         return remote(load.at[partner(k), :, part], arrived.at[slot, :, part], column_sem,
-                      (pieces * GROUPS, k), freq=partner(k))
+                      (offsets[pieces], k), freq=partner(k))
+
+    sent = [(p, n) for p in range(pieces) for n in range(len(cuts[p]) - 1)]
 
     def keep_copy():
         return pltpu.make_async_copy(load.at[me], arrived.at[me], local_sem.at[pieces])
@@ -172,6 +176,18 @@
     def inner_stress(p, i):
         stress_row(p, i, i - 1)
 
+    def edge_rows(p):
+        @pl.when(has_prev)
+        def _():
+            down_copy(p).wait_recv()
+
+        @pl.when(has_next)
+        def _():
+            up_copy(p).wait_recv()
+
+        stress_row(p, 0, rows - 2)
+        stress_row(p, rows - 1, rows - 1)
+
     def each(first, last, act, p, unroll):
         def body(i, carry):
             act(p, i)
@@ -197,18 +213,19 @@
         def _():
             down_copy(p).start()
 
-        for n in range(GROUPS):
-            first = cuts[n] + (n > 0)
-            last = min(cuts[n + 1] + 1, rows - 1)
+        for n in range(len(cuts[p]) - 1):
+            low, high = cuts[p][n], cuts[p][n + 1]
+            first = low + (n > 0)
+            last = min(high + 1, rows - 1)
             each(first, last, blend_row, p, 2)
             each(first, last, map_row, p, 3)
             if p == 0 and n == 0:
                 for k in range(1, owners):
                     stiff_copy(k, source(k)).wait_recv()
                 bending[...] = stiffs[...].astype(F32)
-            each(cuts[n], cuts[n + 1], inner_stress, p, 2)
+            each(low, high, inner_stress, p, 2)
             for k in far_first:
-                inner_copy(p, n, k, me).start()
+                column_copy(p, n, k, me).start()
 
         @pl.when(has_next)
         def _():
@@ -227,25 +244,17 @@
 
     lax.fori_loop(0, factors.shape[1], table_rows, 0)
 
+    late = pieces - 1
     for p in range(pieces):
-        @pl.when(has_prev)
-        def _():
-            down_copy(p).wait_recv()
-
-        @pl.when(has_next)
-        def _():
-            up_copy(p).wait_recv()
-
-        stress_row(p, 0, rows - 2)
-        stress_row(p, rows - 1, rows - 1)
+        edge_rows(p)
     for k in far_first:
-        outer_copy(k, me).start()
+        edge_copy(k, me).start()
     keep_copy().start()
 
-    def history_pair(q, row, step):
+    def history_rows(q, lines):
         sides = []
-        for at in (q, q + 1):
-            stack = [arrived[:, p, at].reshape(-1, PW) for p in range(pieces)]
+        for at in range(len(lines)):
+            stack = [arrived[:, p, q + at].reshape(-1, PW) for p in range(pieces)]
             sides.append(stack[0] if pieces == 1 else jnp.concatenate(stack, 0))
         sides = jnp.concatenate(sides, 1)
         depth = sides.shape[0]
@@ -254,26 +263,35 @@
             part = table[n * per:(n + 1) * per].reshape(2 * BLOCK, depth)
             values = jnp.dot(part, sides, preferred_element_type=F32)
             for h in range(2):
-                for side in range(2):
-                    wide_ref[2 * n + h, pl.ds(row + side * step, BLOCK, stride=rows + 1), :] = (
-                        values[h * BLOCK:(h + 1) * BLOCK, side * PW:(side + 1) * PW])
+                for at, line in enumerate(lines):
+                    wide_ref[2 * n + h, pl.ds(line, BLOCK, stride=rows + 1), :] = (
+                        values[h * BLOCK:(h + 1) * BLOCK, at * PW:(at + 1) * PW])
+
+    def wait_columns(p, n):
+        for k in range(1, owners):
+            column_copy(p, n, k, source(k)).wait_recv()
 
     keep_copy().wait()
-    for n in range(GROUPS):
-        for k in range(1, owners):
-            for p in range(pieces):
-                inner_copy(p, n, k, source(k)).wait_recv()
-
-        def inner_pair(m, carry):
-            q = cuts[n] - 1 + 2 * m
-            history_pair(q, q + 1, 1)
+    for p, n in sent:
+        if p < late:
+            wait_columns(p, n)
+    for n in range(len(cuts[late]) - 1):
+        wait_columns(late, n)
+        low, high = cuts[late][n], cuts[late][n + 1]
+        whole = (high - low) // DEEP
+
+        def deep_rows(m, carry):
+            q = low - 1 + DEEP * m
+            history_rows(q, [q + 1 + at for at in range(DEEP)])
             return carry
 
-        lax.fori_loop(0, (cuts[n + 1] - cuts[n]) // 2, inner_pair, 0)
-
+        lax.fori_loop(0, whole, deep_rows, 0)
+        rest = low + whole * DEEP
+        if rest < high:
+            history_rows(rest - 1, list(range(rest, high)))
     for k in range(1, owners):
-        outer_copy(k, source(k)).wait_recv()
-    history_pair(rows - 2, 0, rows - 1)
+        edge_copy(k, source(k)).wait_recv()
+    history_rows(rows - 2, [0, rows - 1])
 
     @pl.when(has_next)
     def _():
@@ -287,10 +305,9 @@
 
     for k in range(1, owners):
         stiff_copy(k, me).wait_send()
-        for p in range(pieces):
-            for n in range(GROUPS):
-                inner_copy(p, n, k, me).wait_send()
-        outer_copy(k, me).wait_send()
+        for p, n in sent:
+            column_copy(p, n, k, me).wait_send()
+        edge_copy(k, me).wait_send()
 
 
 def exchange(panel_map, weights, labels, own, templates, stiffness, groups, owners, patches):
@@ -323,7 +340,7 @@
             dma((2, pieces)),
             dma((2, pieces, 2)),
             dma((2, owners)),
-            dma((2, pieces * GROUPS + 1, owners)),
+            dma((2, (pieces - 1) * (len(FIRST_SHARES) - 1) + len(LAST_SHARES), owners)),
         ] + [pltpu.VMEM((cf, 2 * width), BF16)] * pieces,
         compiler_params=pltpu.CompilerParams(
             vmem_limit_bytes=VMEM_LIMIT, collective_id=0, has_side_effects=True),
@@ -333,27 +350,36 @@
     )(panel_map, weights, labels, own, templates, stiffness)
 
 
-def finish_kernel(scale, gain_ref, zone_ref, wide_ref, out_ref):
+def finish_kernel(scale, gain_ref, zone_ref, wide_ref, out_ref, staged, sem):
     rows = zone_ref.shape[0]
     gain = jnp.zeros(zone_ref.shape, F32)
     for zone in range(gain_ref.shape[0]):
         gain = jnp.where(zone_ref[...] == zone, gain_ref[zone], gain)
     gain = gain * scale
-    block = pl.program_id(0)
-    for t in range(BLOCK):
-        values = wide_ref[block, pl.ds(t * (rows + 1), rows), :]
-        out_ref[t] = (values * gain).astype(BF16)
+    blocks = NT // BLOCK
+
+    def write(n):
+        part = pl.ds(n * BLOCK, BLOCK)
+        return pltpu.make_async_copy(staged.at[part], out_ref.at[part], sem.at[n])
+
+    for n in range(blocks):
+        for t in range(BLOCK):
+            values = wide_ref[n, pl.ds(t * (rows + 1), rows), :]
+            staged[n * BLOCK + t] = (values * gain).astype(BF16)
+        write(n).start()
+    for n in range(blocks):
+        write(n).wait()
 
 
 def finish(wide, zone_gain, zone_ids, scale):
     rows = zone_ids.shape[0]
     return pl.pallas_call(
         functools.partial(finish_kernel, scale),
-        grid=(NT // BLOCK,),
         out_shape=jax.ShapeDtypeStruct((NT, rows, PW), BF16),
         in_specs=[pl.BlockSpec(memory_space=pltpu.SMEM), pl.BlockSpec(memory_space=pltpu.VMEM),
                   pl.BlockSpec(memory_space=pltpu.VMEM)],
-        out_specs=pl.BlockSpec((BLOCK, rows, PW), lambda t: (t, 0, 0)),
+        out_specs=pl.BlockSpec(memory_space=pl.ANY),
+        scratch_shapes=[pltpu.VMEM((NT, rows, PW), BF16), pltpu.SemaphoreType.DMA((NT // BLOCK,))],
         compiler_params=pltpu.CompilerParams(vmem_limit_bytes=FINISH_LIMIT),
         cost_estimate=pl.CostEstimate(
             flops=NT * rows * PW, bytes_accessed=2 * NT * rows * PW, transcendentals=0),

time: 65.3 us -> 63.6 us (0.974)
  Pallas kernels: 64 us -> 62.7 us
    pallas_call x1, Pallas kernels: 5.29 us -> 4.03 us  [finish(): pl.pallas_call(functools.partial(finish_kernel, scale), out_shape=jax.Sha...]
where the time goes in v3:
time: 63.6 us; the launch traced here: 62.7 us
  Pallas kernels  62.7 us (99%)
    pallas_call x1, Pallas kernels, exchange(): pl.pallas_call(functools.partial(exchange_kernel, rows, groups, owners, p...  58.7 us
    pallas_call x1, Pallas kernels, finish(): pl.pallas_call(functools.partial(finish_kernel, scale), out_shape=jax.Sha...  4.03 us

profile of v3, /device:TPU:2, one launch (start us, length us, event | category | flops | bytes accessed | tf_op | source)
XLA Modules:
  0.0 62.7 jit_solution(18229192557260735704)
XLA Ops:
  0.0 0.0 copy-start
  0.0 0.0 copy-start.1
  0.0 58.7 %shard_map.82.wide_ref = f32[8,4224,128]{2,1,0:T(8,128)S(1)} custom-call(s32[4,256]{1,0:T(4,128)} %bitcast.2, f32[4,256]{1,0:T(4,128)} %bitcast.3, s32[256]{0:T(256)} %label_ref.1, bf16[2,16,32768]{2,1,0:T(8,128)(2,1)} %own_ref.1, bf16[4,128,128]{2,1,0:T(8,128)(2,1)} %templates_ref.1, f32[32,128]{1,0:T(8,128)} %stiff_ref.1), custom_call_target="tpu_custom_call" | custom-call | flops 3221225472 | bytes 41943040 | tf_op jit(solution)/shard_map/pallas_call | solution.py:323
  58.7 0.0 copy-done
  58.7 0.0 copy-done.1
  58.7 4.0 %shard_map.83 = bf16[1024,32,128]{2,1,0:T(8,128)(2,1)} custom-call(f32[8]{0:T(128)S(1)} %copy-done.1, s32[32,128]{1,0:T(8,128)S(1)} %copy-done, f32[8,4224,128]{2,1,0:T(8,128)S(1)} %shard_map.82.wide_ref), custom_call_target="tpu_custom_call" | custom-call | flops 4194304 | bytes 8388608 | tf_op jit(solution)/shard_map/pallas_call | solution.py:376
Async XLA Ops:
  0.0 58.7 %copy-start = (s32[32,128]{1,0:T(8,128)S(1)}, s32[32,128]{1,0:T(8,128)}, u32[]{:S(2)}) copy-start(s32[32,128]{1,0:T(8,128)} %zone_ref.1) | copy-start | bytes 49156
  0.0 58.7 %copy-start.1 = (f32[8]{0:T(128)S(1)}, f32[8]{0:T(128)}, u32[]{:S(2)}) copy-start(f32[8]{0:T(128)} %gain_ref.1) | copy-start | bytes 100

commit v4 on v3

--- a/solution.py
+++ b/solution.py
@@ -12,7 +12,7 @@
 PW = 128
 BLOCK = 128
 DEEP = 8
-FIRST_SHARES = (0, 2, 7, 15)
+FIRST_SHARES = (0, 1, 3, 7, 15)
 LAST_SHARES = (0, 7, 15)
 VMEM_LIMIT = 40 * 1024 * 1024
 FINISH_LIMIT = 16 * 1024 * 1024
@@ -43,8 +43,9 @@
             jnp.cos(small), jnp.sin(small))
 
 
-def exchange_kernel(rows, groups, owners, patches, map_ref, weight_ref, label_ref, own_ref,
-                    templates_ref, stiff_ref, wide_ref,
+def exchange_kernel(rows, groups, owners, patches, map_in, weight_in, label_in, own_ref,
+                    templates_in, stiff_in, wide_ref,
+                    map_ref, weight_ref, label_ref, templates_ref, stiff_ref, fetch_sem,
                     blended, spectra, load, arrived, own_stiff, stiffs, bending, stacked, factors, table,
                     local_sem, press_sem, edge_sem, stiff_sem, column_sem, *tables):
     pieces, cf, width = own_ref.shape
@@ -116,8 +117,14 @@
         pl.semaphore_signal(barrier, inc=1, device_id={"patch": patch + 1},
                             device_id_type=pl.DeviceIdType.MESH)
 
+    fetches = [pltpu.make_async_copy(src, dst, fetch_sem.at[n]) for n, (src, dst) in enumerate((
+        (stiff_in, stiff_ref), (map_in, map_ref), (weight_in, weight_ref), (label_in, label_ref),
+        (templates_in, templates_ref)))]
+    for fetch in fetches:
+        fetch.start()
     for p in range(pieces):
         own_copy(p).start()
+    fetches[0].wait()
     own_stiff[...] = stiff_ref[...].astype(BF16)
     pl.semaphore_wait(
         barrier, owners - 1 + has_prev.astype(jnp.int32) + has_next.astype(jnp.int32))
@@ -129,6 +136,8 @@
     for k in range(1, owners):
         stiff_copy(k, me).start()
     stiffs[me] = own_stiff[...]
+    for fetch in fetches[1:]:
+        fetch.wait()
     for kind in range(kinds):
         stacked[:, kind * PW:(kind + 1) * PW] = templates_ref[kind]
 
@@ -201,18 +210,8 @@
         def _():
             pressure_copy(p).wait_recv()
 
-        for act in (blend_row, map_row):
-            act(p, 0)
-            act(p, rows - 1)
-
-        @pl.when(has_prev)
-        def _():
-            up_copy(p).start()
-
-        @pl.when(has_next)
-        def _():
-            down_copy(p).start()
-
+        blend_row(p, 0)
+        map_row(p, 0)
         for n in range(len(cuts[p]) - 1):
             low, high = cuts[p][n], cuts[p][n + 1]
             first = low + (n > 0)
@@ -226,6 +225,18 @@
             each(low, high, inner_stress, p, 2)
             for k in far_first:
                 column_copy(p, n, k, me).start()
+            if n == 0:
+                blend_row(p, rows - 1)
+                map_row(p, rows - 1)
+
+                @pl.when(has_prev)
+                def _():
+                    up_copy(p).start()
+
+                @pl.when(has_next)
+                def _():
+                    down_copy(p).start()
+
 
         @pl.when(has_next)
         def _():
@@ -316,16 +327,21 @@
     kinds = templates.shape[0]
     depth = owners * pieces * cf
     fine = math.isqrt(NT)
-    smem = pl.BlockSpec(memory_space=pltpu.SMEM)
     hbm = pl.BlockSpec(memory_space=pl.ANY)
     vmem = pl.BlockSpec(memory_space=pltpu.VMEM)
     dma = pltpu.SemaphoreType.DMA
     return pl.pallas_call(
         functools.partial(exchange_kernel, rows, groups, owners, patches),
         out_shape=pltpu.VMEM((NT // BLOCK, BLOCK * (rows + 1), PW), F32),
-        in_specs=[smem, smem, smem, hbm, vmem, vmem],
+        in_specs=[hbm] * 6,
         out_specs=vmem,
         scratch_shapes=[
+            pltpu.SMEM(panel_map.shape, jnp.int32),
+            pltpu.SMEM(weights.shape, F32),
+            pltpu.SMEM(labels.shape, jnp.int32),
+            pltpu.VMEM(templates.shape, BF16),
+            pltpu.VMEM(stiffness.shape, F32),
+            dma((5,)),
             pltpu.VMEM((rows, groups, cf, PW), BF16),
             pltpu.VMEM((pieces, rows + 2, groups, cf, PW), BF16),
             pltpu.VMEM((groups, pieces, rows, cf, PW), BF16),

time: 63.6 us -> 62.6 us (0.984)
  Pallas kernels: 62.7 us -> 61.8 us
    pallas_call x1, Pallas kernels: 58.7 us -> 57.7 us  [exchange(): pl.pallas_call(functools.partial(exchange_kernel, rows, groups, owners, p...]
where the time goes in v4:
time: 62.6 us; the launch traced here: 61.8 us
  Pallas kernels  61.8 us (99%)
    pallas_call x1, Pallas kernels, exchange(): pl.pallas_call(functools.partial(exchange_kernel, rows, groups, owners, p...  57.7 us
    pallas_call x1, Pallas kernels, finish(): pl.pallas_call(functools.partial(finish_kernel, scale), out_shape=jax.Sha...  4.03 us

profile of v4, /device:TPU:2, one launch (start us, length us, event | category | flops | bytes accessed | tf_op | source)
XLA Modules:
  0.0 61.8 jit_solution(14569157108311273000)
XLA Ops:
  0.0 0.0 copy-start
  0.0 0.0 copy-start.1
  0.0 57.7 %shard_map.82.wide_ref = f32[8,4224,128]{2,1,0:T(8,128)S(1)} custom-call(s32[4,256]{1,0:T(4,128)} %bitcast.2, f32[4,256]{1,0:T(4,128)} %bitcast.3, s32[256]{0:T(256)} %label_in.1, bf16[2,16,32768]{2,1,0:T(8,128)(2,1)} %own_ref.1, bf16[4,128,128]{2,1,0:T(8,128)(2,1)} %templates_in.1, f32[32,128]{1,0:T(8,128)} %stiff_in.1), custom_call_target="tpu_custom_call" | custom-call | flops 3221225472 | bytes 41943040 | tf_op jit(solution)/shard_map/pallas_call | solution.py:333
  57.7 0.0 copy-done
  57.8 0.0 copy-done.1
  57.8 4.0 %shard_map.83 = bf16[1024,32,128]{2,1,0:T(8,128)(2,1)} custom-call(f32[8]{0:T(128)S(1)} %copy-done.1, s32[32,128]{1,0:T(8,128)S(1)} %copy-done, f32[8,4224,128]{2,1,0:T(8,128)S(1)} %shard_map.82.wide_ref), custom_call_target="tpu_custom_call" | custom-call | flops 4194304 | bytes 8388608 | tf_op jit(solution)/shard_map/pallas_call | solution.py:392
Async XLA Ops:
  0.0 57.7 %copy-start = (s32[32,128]{1,0:T(8,128)S(1)}, s32[32,128]{1,0:T(8,128)}, u32[]{:S(2)}) copy-start(s32[32,128]{1,0:T(8,128)} %zone_ref.1) | copy-start | bytes 49156
  0.0 57.8 %copy-start.1 = (f32[8]{0:T(128)S(1)}, f32[8]{0:T(128)}, u32[]{:S(2)}) copy-start(f32[8]{0:T(128)} %gain_ref.1) | copy-start | bytes 100

commit v5 on v4

--- a/solution.py
+++ b/solution.py
@@ -52,6 +52,7 @@
     kinds = templates_ref.shape[0]
     me, patch = lax.axis_index("freq"), lax.axis_index("patch")
     has_prev, has_next = patch > 0, patch < patches - 1
+    by_owner = patch < patches // 2
     lane = lax.broadcasted_iota(jnp.int32, (groups, cf, PW), 2)
     empty = jnp.zeros((1, cf, PW), F32)
     cuts = [row_cuts(rows, LAST_SHARES if p == pieces - 1 else FIRST_SHARES) for p in range(pieces)]
@@ -223,8 +224,14 @@
                     stiff_copy(k, source(k)).wait_recv()
                 bending[...] = stiffs[...].astype(F32)
             each(low, high, inner_stress, p, 2)
-            for k in far_first:
-                column_copy(p, n, k, me).start()
+            if p < pieces - 1:
+                for k in far_first:
+                    column_copy(p, n, k, me).start()
+            else:
+                @pl.when(jnp.logical_not(by_owner))
+                def _():
+                    for k in far_first:
+                        column_copy(p, n, k, me).start()
             if n == 0:
                 blend_row(p, rows - 1)
                 map_row(p, rows - 1)
@@ -258,8 +265,19 @@
     late = pieces - 1
     for p in range(pieces):
         edge_rows(p)
-    for k in far_first:
-        edge_copy(k, me).start()
+
+    @pl.when(by_owner)
+    def _():
+        for k in far_first:
+            for n in range(len(cuts[late]) - 1):
+                column_copy(late, n, k, me).start()
+            edge_copy(k, me).start()
+
+    @pl.when(jnp.logical_not(by_owner))
+    def _():
+        for k in far_first:
+            edge_copy(k, me).start()
+
     keep_copy().start()
 
     def history_rows(q, lines):
@@ -372,18 +390,19 @@
     for zone in range(gain_ref.shape[0]):
         gain = jnp.where(zone_ref[...] == zone, gain_ref[zone], gain)
     gain = gain * scale
-    blocks = NT // BLOCK
-
     def write(n):
-        part = pl.ds(n * BLOCK, BLOCK)
-        return pltpu.make_async_copy(staged.at[part], out_ref.at[part], sem.at[n])
-
-    for n in range(blocks):
+        return pltpu.make_async_copy(
+            staged.at[n], out_ref.at[pl.ds(n * BLOCK, BLOCK)], sem.at[n])
+
+    def block(n, carry):
         for t in range(BLOCK):
             values = wide_ref[n, pl.ds(t * (rows + 1), rows), :]
-            staged[n * BLOCK + t] = (values * gain).astype(BF16)
+            staged[n, t] = (values * gain).astype(BF16)
         write(n).start()
-    for n in range(blocks):
+        return carry
+
+    lax.fori_loop(0, NT // BLOCK, block, 0)
+    for n in range(NT // BLOCK):
         write(n).wait()
 
 
@@ -395,7 +414,7 @@
         in_specs=[pl.BlockSpec(memory_space=pltpu.SMEM), pl.BlockSpec(memory_space=pltpu.VMEM),
                   pl.BlockSpec(memory_space=pltpu.VMEM)],
         out_specs=pl.BlockSpec(memory_space=pl.ANY),
-        scratch_shapes=[pltpu.VMEM((NT, rows, PW), BF16), pltpu.SemaphoreType.DMA((NT // BLOCK,))],
+        scratch_shapes=[pltpu.VMEM((NT // BLOCK, BLOCK, rows, PW), BF16), pltpu.SemaphoreType.DMA((NT // BLOCK,))],
         compiler_params=pltpu.CompilerParams(vmem_limit_bytes=FINISH_LIMIT),
         cost_estimate=pl.CostEstimate(
             flops=NT * rows * PW, bytes_accessed=2 * NT * rows * PW, transcendentals=0),

time: 62.6 us -> 61.9 us (0.989); the launches traced: 61.8 us -> 61.8 us
  no operation moved by 1% of the time
where the time goes in v5:
time: 61.9 us; the launch traced here: 61.8 us
  Pallas kernels  61.8 us (100%)
    pallas_call x1, Pallas kernels, exchange(): pl.pallas_call(functools.partial(exchange_kernel, rows, groups, owners, p...  57.8 us
    pallas_call x1, Pallas kernels, finish(): pl.pallas_call(functools.partial(finish_kernel, scale), out_shape=jax.Sha...  4.03 us

profile of v5, /device:TPU:2, one launch (start us, length us, event | category | flops | bytes accessed | tf_op | source)
XLA Modules:
  0.0 61.8 jit_solution(988608308726367386)
XLA Ops:
  0.0 0.0 copy-start
  0.0 0.0 copy-start.1
  0.0 57.8 %shard_map.82.wide_ref = f32[8,4224,128]{2,1,0:T(8,128)S(1)} custom-call(s32[4,256]{1,0:T(4,128)} %bitcast.2, f32[4,256]{1,0:T(4,128)} %bitcast.3, s32[256]{0:T(256)} %label_in.1, bf16[2,16,32768]{2,1,0:T(8,128)(2,1)} %own_ref.1, bf16[4,128,128]{2,1,0:T(8,128)(2,1)} %templates_in.1, f32[32,128]{1,0:T(8,128)} %stiff_in.1), custom_call_target="tpu_custom_call" | custom-call | flops 3221225472 | bytes 41943040 | tf_op jit(solution)/shard_map/pallas_call | solution.py:351
  57.8 0.0 copy-done
  57.8 0.0 copy-done.1
  57.8 4.0 %shard_map.83 = bf16[1024,32,128]{2,1,0:T(8,128)(2,1)} custom-call(f32[8]{0:T(128)S(1)} %copy-done.1, s32[32,128]{1,0:T(8,128)S(1)} %copy-done, f32[8,4224,128]{2,1,0:T(8,128)S(1)} %shard_map.82.wide_ref), custom_call_target="tpu_custom_call" | custom-call | flops 4194304 | bytes 8388608 | tf_op jit(solution)/shard_map/pallas_call | solution.py:411
Async XLA Ops:
  0.0 57.8 %copy-start = (s32[32,128]{1,0:T(8,128)S(1)}, s32[32,128]{1,0:T(8,128)}, u32[]{:S(2)}) copy-start(s32[32,128]{1,0:T(8,128)} %zone_ref.1) | copy-start | bytes 49156
  0.0 57.8 %copy-start.1 = (f32[8]{0:T(128)S(1)}, f32[8]{0:T(128)}, u32[]{:S(2)}) copy-start(f32[8]{0:T(128)} %gain_ref.1) | copy-start | bytes 100

commit v6 on v5

--- a/solution.py
+++ b/solution.py
@@ -12,7 +12,7 @@
 PW = 128
 BLOCK = 128
 DEEP = 8
-FIRST_SHARES = (0, 1, 3, 7, 15)
+FIRST_SHARES = (0, 1, 3, 6, 10, 15)
 LAST_SHARES = (0, 7, 15)
 VMEM_LIMIT = 40 * 1024 * 1024
 FINISH_LIMIT = 16 * 1024 * 1024
@@ -251,6 +251,24 @@
             if p + 1 < pieces:
                 pressure_copy(p + 1).start()
 
+    late = pieces - 1
+    for p in range(pieces):
+        edge_rows(p)
+
+    @pl.when(by_owner)
+    def _():
+        for k in far_first:
+            for n in range(len(cuts[late]) - 1):
+                column_copy(late, n, k, me).start()
+            edge_copy(k, me).start()
+
+    @pl.when(jnp.logical_not(by_owner))
+    def _():
+        for k in far_first:
+            edge_copy(k, me).start()
+
+    keep_copy().start()
+
     for n, values in enumerate(
             fourier_factors(NT, factors.shape[1], factors.shape[2] // 2, cf * pieces // 2, pieces == 2)):
         factors[n] = values
@@ -262,23 +280,6 @@
 
     lax.fori_loop(0, factors.shape[1], table_rows, 0)
 
-    late = pieces - 1
-    for p in range(pieces):
-        edge_rows(p)
-
-    @pl.when(by_owner)
-    def _():
-        for k in far_first:
-            for n in range(len(cuts[late]) - 1):
-                column_copy(late, n, k, me).start()
-            edge_copy(k, me).start()
-
-    @pl.when(jnp.logical_not(by_owner))
-    def _():
-        for k in far_first:
-            edge_copy(k, me).start()
-
-    keep_copy().start()
 
     def history_rows(q, lines):
         sides = []
@@ -350,7 +351,7 @@
     dma = pltpu.SemaphoreType.DMA
     return pl.pallas_call(
         functools.partial(exchange_kernel, rows, groups, owners, patches),
-        out_shape=pltpu.VMEM((NT // BLOCK, BLOCK * (rows + 1), PW), F32),
+        out_shape=pltpu.VMEM((NT // BLOCK, (BLOCK + 1) * (rows + 1), PW), F32),
         in_specs=[hbm] * 6,
         out_specs=vmem,
         scratch_shapes=[

time: 61.9 us -> 61.8 us (level)
  no operation moved by 1% of the time
where the time goes in v6:
time: 61.8 us; the launch traced here: 61.7 us
  Pallas kernels  61.7 us (100%)
    pallas_call x1, Pallas kernels, exchange(): pl.pallas_call(functools.partial(exchange_kernel, rows, groups, owners, p...  57.6 us
    pallas_call x1, Pallas kernels, finish(): pl.pallas_call(functools.partial(finish_kernel, scale), out_shape=jax.Sha...  4.03 us

profile of v6, /device:TPU:2, one launch (start us, length us, event | category | flops | bytes accessed | tf_op | source)
XLA Modules:
  0.0 61.7 jit_solution(8409509061071222048)
XLA Ops:
  0.0 0.0 copy-start
  0.0 0.0 copy-start.1
  0.0 57.6 %shard_map.82.wide_ref = f32[8,4257,128]{2,1,0:T(8,128)S(1)} custom-call(s32[4,256]{1,0:T(4,128)} %bitcast.2, f32[4,256]{1,0:T(4,128)} %bitcast.3, s32[256]{0:T(256)} %label_in.1, bf16[2,16,32768]{2,1,0:T(8,128)(2,1)} %own_ref.1, bf16[4,128,128]{2,1,0:T(8,128)(2,1)} %templates_in.1, f32[32,128]{1,0:T(8,128)} %stiff_in.1), custom_call_target="tpu_custom_call" | custom-call | flops 3221225472 | bytes 41943040 | tf_op jit(solution)/shard_map/pallas_call | solution.py:352
  57.7 0.0 copy-done
  57.7 0.0 copy-done.1
  57.7 4.0 %shard_map.83 = bf16[1024,32,128]{2,1,0:T(8,128)(2,1)} custom-call(f32[8]{0:T(128)S(1)} %copy-done.1, s32[32,128]{1,0:T(8,128)S(1)} %copy-done, f32[8,4257,128]{2,1,0:T(8,128)S(1)} %shard_map.82.wide_ref), custom_call_target="tpu_custom_call" | custom-call | flops 4194304 | bytes 8388608 | tf_op jit(solution)/shard_map/pallas_call | solution.py:412
Async XLA Ops:
  0.0 57.7 %copy-start = (s32[32,128]{1,0:T(8,128)S(1)}, s32[32,128]{1,0:T(8,128)}, u32[]{:S(2)}) copy-start(s32[32,128]{1,0:T(8,128)} %zone_ref.1) | copy-start | bytes 49156
  0.0 57.7 %copy-start.1 = (f32[8]{0:T(128)S(1)}, f32[8]{0:T(128)}, u32[]{:S(2)}) copy-start(f32[8]{0:T(128)} %gain_ref.1) | copy-start | bytes 100

commit v7 on v6

--- a/solution.py
+++ b/solution.py
@@ -43,9 +43,9 @@
             jnp.cos(small), jnp.sin(small))
 
 
-def exchange_kernel(rows, groups, owners, patches, map_in, weight_in, label_in, own_ref,
-                    templates_in, stiff_in, wide_ref,
-                    map_ref, weight_ref, label_ref, templates_ref, stiff_ref, fetch_sem,
+def exchange_kernel(rows, groups, owners, patches, scale, map_in, weight_in, label_in, own_ref,
+                    templates_in, stiff_in, zone_in, gain_in, wide_ref, field_ref,
+                    map_ref, weight_ref, label_ref, templates_ref, stiff_ref, zone_ref, gain_ref, fetch_sem,
                     blended, spectra, load, arrived, own_stiff, stiffs, bending, stacked, factors, table,
                     local_sem, press_sem, edge_sem, stiff_sem, column_sem, *tables):
     pieces, cf, width = own_ref.shape
@@ -120,7 +120,7 @@
 
     fetches = [pltpu.make_async_copy(src, dst, fetch_sem.at[n]) for n, (src, dst) in enumerate((
         (stiff_in, stiff_ref), (map_in, map_ref), (weight_in, weight_ref), (label_in, label_ref),
-        (templates_in, templates_ref)))]
+        (templates_in, templates_ref), (zone_in, zone_ref), (gain_in, gain_ref)))]
     for fetch in fetches:
         fetch.start()
     for p in range(pieces):
@@ -269,6 +269,11 @@
 
     keep_copy().start()
 
+    gain = jnp.zeros(zone_ref.shape, F32)
+    for zone in range(gain_ref.shape[0]):
+        gain = jnp.where(zone_ref[...] == zone, gain_ref[zone], gain)
+    field_ref[...] = gain * scale
+
     for n, values in enumerate(
             fourier_factors(NT, factors.shape[1], factors.shape[2] // 2, cf * pieces // 2, pieces == 2)):
         factors[n] = values
@@ -340,7 +345,7 @@
         edge_copy(k, me).wait_send()
 
 
-def exchange(panel_map, weights, labels, own, templates, stiffness, groups, owners, patches):
+def exchange(panel_map, weights, labels, own, templates, stiffness, zone_ids, zone_gain, scale, groups, owners, patches):
     rows = stiffness.shape[0]
     pieces, cf, width = own.shape
     kinds = templates.shape[0]
@@ -350,17 +355,20 @@
     vmem = pl.BlockSpec(memory_space=pltpu.VMEM)
     dma = pltpu.SemaphoreType.DMA
     return pl.pallas_call(
-        functools.partial(exchange_kernel, rows, groups, owners, patches),
-        out_shape=pltpu.VMEM((NT // BLOCK, (BLOCK + 1) * (rows + 1), PW), F32),
-        in_specs=[hbm] * 6,
-        out_specs=vmem,
+        functools.partial(exchange_kernel, rows, groups, owners, patches, scale),
+        out_shape=(pltpu.VMEM((NT // BLOCK, (BLOCK + 1) * (rows + 1), PW), F32),
+                   pltpu.VMEM((rows, PW), F32)),
+        in_specs=[hbm] * 8,
+        out_specs=(vmem, vmem),
         scratch_shapes=[
             pltpu.SMEM(panel_map.shape, jnp.int32),
             pltpu.SMEM(weights.shape, F32),
             pltpu.SMEM(labels.shape, jnp.int32),
             pltpu.VMEM(templates.shape, BF16),
             pltpu.VMEM(stiffness.shape, F32),
-            dma((5,)),
+            pltpu.VMEM(zone_ids.shape, jnp.int32),
+            pltpu.SMEM(zone_gain.shape, F32),
+            dma((7,)),
             pltpu.VMEM((rows, groups, cf, PW), BF16),
             pltpu.VMEM((pieces, rows + 2, groups, cf, PW), BF16),
             pltpu.VMEM((groups, pieces, rows, cf, PW), BF16),
@@ -382,15 +390,13 @@
         cost_estimate=pl.CostEstimate(
             flops=2 * own.size * kinds * PW + 2 * NT * depth * rows * PW,
             bytes_accessed=40 * own.size, transcendentals=0),
-    )(panel_map, weights, labels, own, templates, stiffness)
-
-
-def finish_kernel(scale, gain_ref, zone_ref, wide_ref, out_ref, staged, sem):
-    rows = zone_ref.shape[0]
-    gain = jnp.zeros(zone_ref.shape, F32)
-    for zone in range(gain_ref.shape[0]):
-        gain = jnp.where(zone_ref[...] == zone, gain_ref[zone], gain)
-    gain = gain * scale
+    )(panel_map, weights, labels, own, templates, stiffness, zone_ids, zone_gain)
+
+
+def finish_kernel(field_ref, wide_ref, out_ref, staged, sem):
+    rows = field_ref.shape[0]
+    gain = field_ref[...]
+
     def write(n):
         return pltpu.make_async_copy(
             staged.at[n], out_ref.at[pl.ds(n * BLOCK, BLOCK)], sem.at[n])
@@ -407,19 +413,18 @@
         write(n).wait()
 
 
-def finish(wide, zone_gain, zone_ids, scale):
-    rows = zone_ids.shape[0]
+def finish(wide, field):
+    rows = field.shape[0]
     return pl.pallas_call(
-        functools.partial(finish_kernel, scale),
+        finish_kernel,
         out_shape=jax.ShapeDtypeStruct((NT, rows, PW), BF16),
-        in_specs=[pl.BlockSpec(memory_space=pltpu.SMEM), pl.BlockSpec(memory_space=pltpu.VMEM),
-                  pl.BlockSpec(memory_space=pltpu.VMEM)],
+        in_specs=[pl.BlockSpec(memory_space=pltpu.VMEM)] * 2,
         out_specs=pl.BlockSpec(memory_space=pl.ANY),
         scratch_shapes=[pltpu.VMEM((NT // BLOCK, BLOCK, rows, PW), BF16), pltpu.SemaphoreType.DMA((NT // BLOCK,))],
         compiler_params=pltpu.CompilerParams(vmem_limit_bytes=FINISH_LIMIT),
         cost_estimate=pl.CostEstimate(
             flops=NT * rows * PW, bytes_accessed=2 * NT * rows * PW, transcendentals=0),
-    )(zone_gain, zone_ids, pltpu.with_memory_space_constraint(wide, pltpu.VMEM))
+    )(*(pltpu.with_memory_space_constraint(x, pltpu.VMEM) for x in (field, wide)))
 
 
 def shards(
@@ -433,10 +438,10 @@
 
     pieces = 2 if fl % 16 == 0 else 1
     own = pressures.reshape(pieces, 2 * fl // pieces, pressures.shape[2])
-    wide = exchange(
-        panel_map.T, blend_weights.T, pattern_label, own, templates, stiffness, groups, owners,
-        lax.axis_size("patch"))
-    return finish(wide, zone_gain, zone_ids, 1.0 / math.sqrt(nfreq))
+    wide, field = exchange(
+        panel_map.T, blend_weights.T, pattern_label, own, templates, stiffness, zone_ids, zone_gain,
+        1.0 / math.sqrt(nfreq), groups, owners, lax.axis_size("patch"))
+    return finish(wide, field)
 
 
 def solution(mesh):

time: 61.8 us -> 61.3 us (level)
  no operation moved by 1% of the time
where the time goes in v7:
time: 61.3 us; the launch traced here: 61.1 us
  Pallas kernels  61.1 us (100%)
    pallas_call x1, Pallas kernels, exchange(): pl.pallas_call(functools.partial(exchange_kernel, rows, groups, owners, p...  57.6 us
    pallas_call x1, Pallas kernels, finish(): pl.pallas_call(finish_kernel, out_shape=jax.ShapeDtypeStruct((NT, rows, P...  3.48 us

profile of v7, /device:TPU:2, one launch (start us, length us, event | category | flops | bytes accessed | tf_op | source)
XLA Modules:
  0.0 61.1 jit_solution(671491132633817308)
XLA Ops:
  0.0 57.6 %shard_map.82 = (f32[8,4257,128]{2,1,0:T(8,128)S(1)}, f32[32,128]{1,0:T(8,128)S(1)}) custom-call(s32[4,256]{1,0:T(4,128)} %bitcast.2, f32[4,256]{1,0:T(4,128)} %bitcast.3, s32[256]{0:T(256)} %label_in.1, bf16[2,16,32768]{2,1,0:T(8,128)(2,1)} %own_ref.1, bf16[4,128,128]{2,1,0:T(8,128)(2,1)} %templates_in.1, f32[32,128]{1,0:T(8,128)} %stiff_in.1, ...), custom_call_target="tpu_custom_call" | custom-call | flops 3221225472 | bytes 41943040 | tf_op jit(solution)/shard_map/pallas_call | solution.py:357
  57.6 3.5 %shard_map.83 = bf16[1024,32,128]{2,1,0:T(8,128)(2,1)} custom-call(f32[32,128]{1,0:T(8,128)S(1)} %get-tuple-element.7.field_ref, f32[8,4257,128]{2,1,0:T(8,128)S(1)} %get-tuple-element.8.wide_ref), custom_call_target="tpu_custom_call" | custom-call | flops 4194304 | bytes 8388608 | tf_op jit(solution)/shard_map/pallas_call | solution.py:418
